TPU v7x, 32 devices: a whole 2x2x4 slice. The times are simulated.
32 devices in a mesh: group: 8 (over y, x, core), dom: 4 (over z).
Axes of the slice: x: 2, y: 2, z: 4, core: 2. Of those that a mesh axis runs over, the one named last changes fastest.
Arguments:
- x_self: bfloat16 [32768, 256], P(('group', 'dom')), may hold values from -6 to 6
- x_src: bfloat16 [16384, 256], P(('group', 'dom')), may hold values from -6 to 6
- tiles: bfloat16 [768, 128, 128], P(('group', 'dom')), may hold values from -0.375 to 0.375
- slot_dest_row: int32 [768], P(('group', 'dom')), may hold values from 0 to 11
- block_col: int32 [768], P(('group', 'dom')), may hold values from 0 to 3
- block_count: int32 [32], P(('group', 'dom')), may hold values from 2 to 24, as said below
- mirror_count: int32 [32, 4], P(('group', 'dom')), may hold values from 0 to 128, as said below
- mirror_index: int32 [32, 4, 128], P(('group', 'dom')), may hold values from 0 to 1023
- cotangent: bfloat16 [32768, 256], P(('group', 'dom')), may hold values from -6 to 6
- w_self: bfloat16 [256, 256], replicated, may hold values from -0.375 to 0.375
- w_neigh: bfloat16 [256, 256], replicated, may hold values from -0.375 to 0.375
Outputs:
- out: bfloat16 [32768, 256], P(('group', 'dom'))
- dx_self: bfloat16 [32768, 256], P(('group', 'dom'))
- dx_src: bfloat16 [16384, 256], P(('group', 'dom'))
- grad_weight: float32 [512, 256], P('group')
Inputs may be any that keep to these rules, and one draw needn't show every extreme that they name: `block_count`: at least 2 and at most 24 tile slots of a device are live; some device has all 24 live. `mirror_count`: at most 128 live rows from one peer; on some device every peer sends 128.
All inputs are finite; a program needn't handle non-finite values.
Results may differ from a plain program's by a relative error of at most 0.02.
Values may be sent and summed in bfloat16 or wider, within the bound.
A program may use at most 64 MiB of HBM per device.

v0:
```python
import functools

import jax
import jax.numpy as jnp
from jax import lax
from jax.experimental import pallas as pl
from jax.experimental.pallas import tpu as pltpu
from jax.sharding import PartitionSpec as P

TILE_EDGE = 128
VMEM_LIMIT = 63 * 2**20
MESH = pl.DeviceIdType.MESH
F32 = jnp.float32
BF16 = jnp.bfloat16


def dot(a, b):
    return jnp.dot(a, b, preferred_element_type=F32)


def dot_nt(a, b):
    return lax.dot_general(a, b, (((1,), (1,)), ((), ())), preferred_element_type=F32)


def adjacency_kernel(
    masters,
    dest_ref,
    col_ref,
    count_ref,
    tiles_hbm,
    x_src_hbm,
    adj_ref,
    mirror_ref,
    tiles_ref,
    x_src_ref,
    sums,
    load_sem,
):
    src_count = x_src_ref.shape[0] // TILE_EDGE
    row_tiles = adj_ref.shape[0] // TILE_EDGE
    load_tiles = pltpu.make_async_copy(tiles_hbm, tiles_ref, load_sem.at[0])
    load_tiles.start()
    load_src = pltpu.make_async_copy(x_src_hbm, x_src_ref, load_sem.at[1])
    load_src.start()
    sums[...] = jnp.zeros_like(sums)
    load_tiles.wait()
    load_src.wait()

    @pl.loop(0, count_ref[0])
    def _(b):
        at = dest_ref[b] * src_count + col_ref[b]
        sums[at] += tiles_ref[b].astype(F32)

    @pl.loop(0, row_tiles)
    def _(t):
        rows = pl.ds(pl.multiple_of(t * TILE_EDGE, TILE_EDGE), TILE_EDGE)
        for s in range(src_count):
            adj_ref[rows, s * TILE_EDGE : (s + 1) * TILE_EDGE] = sums[t * src_count + s].astype(BF16)

    mirror_ref[...] = dot(adj_ref[masters:, :], x_src_ref[...]).astype(BF16)


def layer_kernel(
    ndom,
    ngroup,
    capacity,
    factor,
    live_ref,
    index_hbm,
    adj_hbm,
    mirror_ref,
    x_self_hbm,
    x_src_hbm,
    cot_hbm,
    w_self_hbm,
    w_neigh_hbm,
    out_hbm,
    dx_self_hbm,
    dx_src_hbm,
    grad_ref,
    out,
    dx_self,
    dx_src,
    index3,
    index,
    adj,
    x_self,
    x_src,
    cot,
    w_self,
    w_neigh,
    adj_t,
    pick,
    pick_t,
    own,
    pre_self,
    agg,
    gpre,
    g_agg,
    dx_acc,
    received,
    back,
    mirror_grad,
    x_self_t,
    term,
    term_in,
    rows_out,
    rows_in,
    load_sem,
    store_sem,
    local_sem,
    send_a,
    recv_a,
    send_b,
    recv_b,
    send_g,
    recv_g,
    send_d,
    recv_d,
):
    me_d = lax.axis_index("dom")
    me_g = lax.axis_index("group")
    masters, width = x_self.shape
    slots = index.shape[1]
    nsrc = x_src.shape[0]
    grad_rows = term.shape[0] // ngroup
    chunk = 256

    barrier = pltpu.get_barrier_semaphore()
    for k in range(1, ndom):
        pl.semaphore_signal(
            barrier, inc=1, device_id={"dom": lax.rem(me_d + k, ndom)}, device_id_type=MESH
        )
    for k in range(1, ngroup):
        pl.semaphore_signal(
            barrier, inc=1, device_id={"group": lax.rem(me_g + k, ngroup)}, device_id_type=MESH
        )
    loads = [
        pltpu.make_async_copy(src, dst, load_sem.at[i])
        for i, (src, dst) in enumerate(
            [
                (index_hbm, index3),
                (x_self_hbm, x_self),
                (w_self_hbm, w_self),
                (x_src_hbm, x_src),
                (adj_hbm, adj),
                (w_neigh_hbm, w_neigh),
                (cot_hbm, cot),
            ]
        )
    ]
    for load in loads:
        load.start()
    pl.semaphore_wait(barrier, ndom + ngroup - 2)

    def part(ref, i, rows):
        return ref.at[pl.ds(pl.multiple_of(i * rows, 16), rows), :]

    def exchange(src, dst, rows, size, me, axis, send, recv):
        copies = []
        for k in range(1, size):
            to = lax.rem(me + k, size)
            copy = pltpu.make_async_remote_copy(
                src_ref=part(src, to, rows) if src is not rows_out else src,
                dst_ref=part(dst, me, rows),
                send_sem=send.at[k],
                recv_sem=recv.at[k],
                device_id={axis: to},
                device_id_type=MESH,
            )
            copy.start()
            copies.append(copy)
        return copies

    sent_a = exchange(mirror_ref, received, capacity, ndom, me_d, "dom", send_a, recv_a)
    keep_a = pltpu.make_async_copy(
        part(mirror_ref, me_d, capacity), part(received, me_d, capacity), local_sem.at[0]
    )
    keep_a.start()

    for load in loads:
        load.wait()
    lane = lax.broadcasted_iota(jnp.int32, (1, capacity), 1)
    for p in range(ndom):
        index[:, p * capacity : (p + 1) * capacity] = jnp.where(
            lane < live_ref[0, p], index3[0, p : p + 1, :], -1
        )
    index_row = index[...]

    @pl.loop(0, masters // chunk)
    def _(i):
        rows = pl.ds(pl.multiple_of(i * chunk, chunk), chunk)
        own[rows, :] = dot(adj[rows, :], x_src[...])
        pre_self[rows, :] = dot(x_self[rows, :], w_self[...])
        ids = lax.broadcasted_iota(jnp.int32, (chunk, slots), 0) + i * chunk
        pick[rows, :] = jnp.where(ids == index_row, 1.0, 0.0).astype(BF16)

    index_col = jnp.broadcast_to(index_row, (TILE_EDGE, slots)).T
    lanes = lax.broadcasted_iota(jnp.int32, (slots, TILE_EDGE), 1)
    for k in range(masters // TILE_EDGE):
        pick_t[:, k * TILE_EDGE : (k + 1) * TILE_EDGE] = jnp.where(
            lanes + k * TILE_EDGE == index_col, 1.0, 0.0
        ).astype(BF16)
    for k in range(masters // chunk):
        x_self_t[:, k * chunk : (k + 1) * chunk] = x_self[k * chunk : (k + 1) * chunk, :].T

    keep_a.wait()
    for copy in sent_a:
        copy.wait()

    for i in range(masters // chunk):
        rows = pl.ds(i * chunk, chunk)
        agg_rows = (own[rows, :] + dot(pick[rows, :], received[...])).astype(BF16)
        agg[rows, :] = agg_rows
        pre = pre_self[rows, :] + dot(agg_rows, w_neigh[...])
        s = jax.nn.sigmoid(pre)
        out[rows, :] = (pre * s).astype(BF16)
        g = (cot[rows, :].astype(F32) * s * (1.0 + pre * (1.0 - s))).astype(BF16)
        gpre[rows, :] = g
        g_agg[rows, :] = dot_nt(g, w_neigh[...]).astype(BF16)

    store_out = pltpu.make_async_copy(out, out_hbm, store_sem.at[0])
    store_out.start()

    term[:width, :] = dot(x_self_t[...], gpre[...]).astype(BF16)
    term[width:, :] = lax.dot_general(
        agg[...], gpre[...], (((0,), (0,)), ((), ())), preferred_element_type=F32
    ).astype(BF16)
    sent_g = exchange(term, term_in, grad_rows, ngroup, me_g, "group", send_g, recv_g)
    keep_g = pltpu.make_async_copy(
        part(term, me_g, grad_rows), part(term_in, me_g, grad_rows), local_sem.at[2]
    )
    keep_g.start()

    back[...] = dot(pick_t[...], g_agg[...]).astype(BF16)
    sent_b = exchange(back, mirror_grad, capacity, ndom, me_d, "dom", send_b, recv_b)
    keep_b = pltpu.make_async_copy(
        part(back, me_d, capacity), part(mirror_grad, me_d, capacity), local_sem.at[1]
    )
    keep_b.start()

    @pl.loop(0, masters // chunk)
    def _(i):
        rows = pl.ds(pl.multiple_of(i * chunk, chunk), chunk)
        dx_self[rows, :] = dot_nt(gpre[rows, :], w_self[...]).astype(BF16)

    store_dx_self = pltpu.make_async_copy(dx_self, dx_self_hbm, store_sem.at[1])
    store_dx_self.start()

    for k in range(masters // chunk):
        adj_t[:, k * chunk : (k + 1) * chunk] = adj[k * chunk : (k + 1) * chunk, :].T

    keep_g.wait()
    for copy in sent_g:
        copy.wait()
    total = term_in[:grad_rows, :].astype(F32)
    for j in range(1, ngroup):
        total = total + term_in[j * grad_rows : (j + 1) * grad_rows, :].astype(F32)
    rows_out[...] = total.astype(BF16)
    sent_d = exchange(rows_out, rows_in, grad_rows, ndom, me_d, "dom", send_d, recv_d)
    keep_d = pltpu.make_async_copy(rows_out, part(rows_in, me_d, grad_rows), local_sem.at[3])
    keep_d.start()

    for k in range(masters // chunk, adj.shape[0] // chunk):
        adj_t[:, k * chunk : (k + 1) * chunk] = adj[k * chunk : (k + 1) * chunk, :].T
    dx_acc[...] = dot(adj_t[:, :masters], g_agg[...])
    keep_b.wait()
    for copy in sent_b:
        copy.wait()
    dx_src[...] = (dx_acc[...] + dot(adj_t[:, masters:], mirror_grad[...])).astype(BF16)
    store_dx_src = pltpu.make_async_copy(dx_src, dx_src_hbm, store_sem.at[2])
    store_dx_src.start()

    keep_d.wait()
    for copy in sent_d:
        copy.wait()
    total = rows_in[:grad_rows, :].astype(F32)
    for j in range(1, ndom):
        total = total + rows_in[j * grad_rows : (j + 1) * grad_rows, :].astype(F32)
    grad_ref[...] = total * factor
    store_out.wait()
    store_dx_self.wait()
    store_dx_src.wait()


def results_kernel(*refs):
    sources, targets, stages = refs[:4], refs[4:8], refs[8:12]
    load_sem, store_sem = refs[12:]
    loads = [
        pltpu.make_async_copy(a, b, load_sem.at[i]) for i, (a, b) in enumerate(zip(sources, stages))
    ]
    stores = [
        pltpu.make_async_copy(a, b, store_sem.at[i]) for i, (a, b) in enumerate(zip(stages, targets))
    ]
    for load in loads:
        load.start()
    for load, store in zip(loads, stores):
        load.wait()
        store.start()
    for store in stores:
        store.wait()


def on_device(
    x_self,
    x_src,
    tiles,
    slot_dest_row,
    block_col,
    block_count,
    mirror_count,
    mirror_index,
    cotangent,
    w_self,
    w_neigh,
):
    masters, width = x_self.shape
    nsrc = x_src.shape[0]
    ndom = lax.axis_size("dom")
    ngroup = lax.axis_size("group")
    capacity = mirror_index.shape[2]
    slots = ndom * capacity
    dest = masters + slots
    grad_rows = 2 * width // ngroup
    smem = pl.BlockSpec(memory_space=pltpu.SMEM)
    vmem = pl.BlockSpec(memory_space=pltpu.VMEM)
    anywhere = pl.BlockSpec(memory_space=pl.ANY)
    hbm = pl.BlockSpec(memory_space=pltpu.HBM)

    adj, mirror = pl.pallas_call(
        functools.partial(adjacency_kernel, masters),
        out_shape=(
            jax.ShapeDtypeStruct((dest, nsrc), BF16),
            jax.ShapeDtypeStruct((slots, width), BF16),
        ),
        in_specs=[smem, smem, smem, hbm, hbm],
        out_specs=(vmem, vmem),
        scratch_shapes=[
            pltpu.VMEM(tiles.shape, BF16),
            pltpu.VMEM(x_src.shape, BF16),
            pltpu.VMEM((dest * nsrc // TILE_EDGE**2, TILE_EDGE, TILE_EDGE), F32),
            pltpu.SemaphoreType.DMA((2,)),
        ],
        compiler_params=pltpu.CompilerParams(vmem_limit_bytes=VMEM_LIMIT),
        name="adjacency",
    )(slot_dest_row, block_col, block_count, tiles, x_src)

    factor = float((masters * ngroup * ndom) ** -0.5)

    def rows16(n, m=width):
        return pltpu.VMEM((n, m), BF16)

    def dma(n):
        return pltpu.SemaphoreType.DMA((n,))

    result_shapes = (
        jax.ShapeDtypeStruct((masters, width), BF16),
        jax.ShapeDtypeStruct((masters, width), BF16),
        jax.ShapeDtypeStruct((nsrc, width), BF16),
        jax.ShapeDtypeStruct((grad_rows, width), F32),
    )
    results = pl.pallas_call(
        functools.partial(layer_kernel, ndom, ngroup, capacity, factor),
        out_shape=result_shapes,
        in_specs=[smem, hbm, anywhere, anywhere, hbm, hbm, hbm, hbm, hbm],
        out_specs=(hbm, hbm, hbm, vmem),
        scratch_shapes=[
            rows16(masters),
            rows16(masters),
            rows16(nsrc),
            pltpu.VMEM((1, ndom, capacity), jnp.int32),
            pltpu.VMEM((1, slots), jnp.int32),
            rows16(dest, nsrc),
            rows16(masters),
            rows16(nsrc),
            rows16(masters),
            rows16(width),
            rows16(width),
            rows16(nsrc, dest),
            rows16(masters, slots),
            rows16(slots, masters),
            pltpu.VMEM((masters, width), F32),
            pltpu.VMEM((masters, width), F32),
            rows16(masters),
            rows16(masters),
            rows16(masters),
            pltpu.VMEM((nsrc, width), F32),
            rows16(slots),
            rows16(slots),
            rows16(slots),
            rows16(width, masters),
            rows16(2 * width),
            rows16(2 * width),
            rows16(grad_rows),
            rows16(ndom * grad_rows),
            dma(7),
            dma(3),
            dma(4),
            dma(ndom),
            dma(ndom),
            dma(ndom),
            dma(ndom),
            dma(ngroup),
            dma(ngroup),
            dma(ndom),
            dma(ndom),
        ],
        compiler_params=pltpu.CompilerParams(
            collective_id=0, has_side_effects=True, vmem_limit_bytes=VMEM_LIMIT
        ),
        name="layer",
    )(mirror_count, mirror_index, adj, mirror, x_self, x_src, cotangent, w_self, w_neigh)
    return pl.pallas_call(
        results_kernel,
        out_shape=result_shapes,
        in_specs=[anywhere] * 4,
        out_specs=(hbm,) * 4,
        scratch_shapes=[pltpu.VMEM(shape.shape, shape.dtype) for shape in result_shapes]
        + [dma(4), dma(4)],
        compiler_params=pltpu.CompilerParams(vmem_limit_bytes=VMEM_LIMIT),
        name="results",
    )(*results)


def solution(mesh):
    return jax.shard_map(
        on_device,
        mesh=mesh,
        in_specs=(
            P(("group", "dom"), None),
            P(("group", "dom"), None),
            P(("group", "dom"), None, None),
            P(("group", "dom")),
            P(("group", "dom")),
            P(("group", "dom")),
            P(("group", "dom"), None),
            P(("group", "dom"), None, None),
            P(("group", "dom"), None),
            P(),
            P(),
        ),
        out_specs=(
            P(("group", "dom"), None),
            P(("group", "dom"), None),
            P(("group", "dom"), None),
            P("group", None),
        ),
        check_vma=False,
    )
```

profile of v0, /device:TPU:0, one launch (start us, length us, event | category | flops | bytes accessed | tf_op | source)
XLA Modules:
  0.0 33.1 jit_solution(3315733361585731677)
XLA Ops:
  1.3 3.4 %adjacency.1 = (bf16[1536,512]{1,0:T(8,128)(2,1)}, bf16[512,256]{1,0:T(8,128)(2,1)}) custom-call(s32[24]{0:T(128)} %dest_ref.1, s32[24]{0:T(128)} %col_ref.1, s32[1]{0:T(128)S(6)} %copy.15.count_ref, bf16[24,128,128]{2,1,0:T(8,128)(2,1)} %tiles_hbm.1, bf16[512,256]{1,0:T(8,128)(2,1)} %x_src_hbm.3), custom_call_target="tpu_custom_call" | custom-call | tf_op jit(solution)/shard_map/adjacency/pallas_call | solution.py:330
  4.7 26.2 %layer.1 = (bf16[1024,256]{1,0:T(8,128)(2,1)}, bf16[1024,256]{1,0:T(8,128)(2,1)}, bf16[512,256]{1,0:T(8,128)(2,1)}, f32[64,256]{1,0:T(8,128)}) custom-call(s32[1,4]{1,0:T(1,128)} %live_ref.1, s32[1,4,128]{2,1,0:T(4,128)} %index_hbm.1, bf16[1536,512]{1,0:T(8,128)(2,1)} %get-tuple-element.10.adj_hbm, bf16[512,256]{1,0:T(8,128)(2,1)} %get-tuple-element.11.mirror_ref, ...), custom_call_target="tpu_custom_call" | custom-call | tf_op jit(solution)/shard_map/layer/pallas_call | solution.py:362
  30.9 2.2 %results.1 = (bf16[1024,256]{1,0:T(8,128)(2,1)}, bf16[1024,256]{1,0:T(8,128)(2,1)}, bf16[512,256]{1,0:T(8,128)(2,1)}, f32[64,256]{1,0:T(8,128)}) custom-call(bf16[1024,256]{1,0:T(8,128)(2,1)} %get-tuple-element.12.refs_0_, bf16[1024,256]{1,0:T(8,128)(2,1)} %get-tuple-element.13.refs_1_, bf16[512,256]{1,0:T(8,128)(2,1)} %get-tuple-element.14.refs_2_, ...), custom_call_target="tpu_custom_call" | custom-call | tf_op jit(solution)/shard_map/results/pallas_call | solution.py:413
where the time goes:
time: 33.3 us; the launch traced here: 33.1 us
  Pallas kernels  31.8 us (95%)
  between operations  1.29 us (4%)
    pallas_call x1, Pallas kernels, on_device(): pl.pallas_call(functools.partial(layer_kernel, ndom, ngroup, capacity, fa...  26.2 us
    pallas_call x1, Pallas kernels, on_device(): pl.pallas_call(functools.partial(adjacency_kernel, masters), out_shape=(j...  3.39 us
    pallas_call x1, Pallas kernels, on_device(): pl.pallas_call(results_kernel, out_shape=result_shapes, in_specs=[anywher...  2.17 us

commit v1 on v0

--- a/solution.py
+++ b/solution.py
@@ -8,7 +8,7 @@
 from jax.sharding import PartitionSpec as P
 
 TILE_EDGE = 128
-VMEM_LIMIT = 63 * 2**20
+VMEM_LIMIT = 24 * 2**20
 MESH = pl.DeviceIdType.MESH
 F32 = jnp.float32
 BF16 = jnp.bfloat16

time: 33.3 us -> 38.4 us (1.15)
  local copies, waits for them, and re-layouts: 0 us -> 8.61 us
  Pallas kernels: 31.8 us -> 28 us
    unnamed x0 -> x20, local copies, waits for them, and re-layouts: none -> 8.61 us
    pallas_call x1, Pallas kernels: 3.39 us -> 1.64 us  [on_device(): pl.pallas_call(functools.partial(adjacency_kernel, masters), out_shape=(j...]
    pallas_call x1, Pallas kernels: 26.2 us -> 25.1 us  [on_device(): pl.pallas_call(functools.partial(layer_kernel, ndom, ngroup, capacity, fa...]
    pallas_call x1, Pallas kernels: 2.17 us -> 1.31 us  [on_device(): pl.pallas_call(results_kernel, out_shape=result_shapes, in_specs=[anywher...]
where the time goes in v1:
time: 38.4 us; the launch traced here: 37.9 us
  Pallas kernels  28 us (73%)
  local copies, waits for them, and re-layouts  8.61 us (22%)
  between operations  1.32 us (3%)
    pallas_call x1, Pallas kernels, on_device(): pl.pallas_call(functools.partial(layer_kernel, ndom, ngroup, capacity, fa...  25.1 us
    unnamed x20, local copies, waits for them, and re-layouts  8.61 us
    pallas_call x1, Pallas kernels, on_device(): pl.pallas_call(functools.partial(adjacency_kernel, masters), out_shape=(j...  1.64 us
    pallas_call x1, Pallas kernels, on_device(): pl.pallas_call(results_kernel, out_shape=result_shapes, in_specs=[anywher...  1.31 us

profile of v1, /device:TPU:0, one launch (start us, length us, event | category | flops | bytes accessed | tf_op | source)
XLA Modules:
  0.0 37.9 jit_solution(10194698923012110104)
XLA Ops:
  1.3 0.0 copy-start
  1.3 0.9 %copy-done = bf16[512,256]{1,0:T(8,128)(2,1)S(1)} copy-done((bf16[512,256]{1,0:T(8,128)(2,1)S(1)}, bf16[512,256]{1,0:T(8,128)(2,1)}, u32[]{:S(2)}) %copy-start) | copy-done | bytes 262168
  2.2 0.0 copy-start.1
  2.2 1.1 %copy-done.1 = bf16[24,128,128]{2,1,0:T(8,128)(2,1)S(1)} copy-done((bf16[24,128,128]{2,1,0:T(8,128)(2,1)S(1)}, bf16[24,128,128]{2,1,0:T(8,128)(2,1)}, u32[]{:S(2)}) %copy-start.1) | copy-done | bytes 786456
  3.4 0.0 copy-start.7
  3.4 0.7 %copy-done.7 = s32[24]{0:T(128)S(1)} copy-done((s32[24]{0:T(128)S(1)}, s32[24]{0:T(128)}, u32[]{:S(2)}) %copy-start.7) | copy-done | bytes 120
  4.0 0.0 copy-start.8
  4.0 0.7 %copy-done.8 = s32[24]{0:T(128)S(1)} copy-done((s32[24]{0:T(128)S(1)}, s32[24]{0:T(128)}, u32[]{:S(2)}) %copy-start.8) | copy-done | bytes 120
  4.7 1.6 %adjacency.1 = (bf16[1536,512]{1,0:T(8,128)(2,1)S(1)}, bf16[512,256]{1,0:T(8,128)(2,1)S(1)}) custom-call(s32[24]{0:T(128)S(1)} %copy-done.7, s32[24]{0:T(128)S(1)} %copy-done.8, s32[1]{0:T(128)S(6)} %copy.15.count_ref, bf16[24,128,128]{2,1,0:T(8,128)(2,1)S(1)} %copy-done.1, bf16[512,256]{1,0:T(8,128)(2,1)S(1)} %copy-done), custom_call_target="tpu_custom_call" | custom-call | tf_op jit(solution)/shard_map/adjacency/pallas_call | solution.py:330
  6.3 0.0 copy-start.2
  6.3 1.0 %copy-done.2 = bf16[1024,256]{1,0:T(8,128)(2,1)S(1)} copy-done((bf16[1024,256]{1,0:T(8,128)(2,1)S(1)}, bf16[1024,256]{1,0:T(8,128)(2,1)}, u32[]{:S(2)}) %copy-start.2) | copy-done | bytes 524312
  7.4 0.0 copy-start.3
  7.4 1.0 %copy-done.3 = bf16[1024,256]{1,0:T(8,128)(2,1)S(1)} copy-done((bf16[1024,256]{1,0:T(8,128)(2,1)S(1)}, bf16[1024,256]{1,0:T(8,128)(2,1)}, u32[]{:S(2)}) %copy-start.3) | copy-done | bytes 524312
  8.4 0.0 copy-start.4
  8.4 0.9 %copy-done.4 = bf16[256,256]{1,0:T(8,128)(2,1)S(1)} copy-done((bf16[256,256]{1,0:T(8,128)(2,1)S(1)}, bf16[256,256]{1,0:T(8,128)(2,1)}, u32[]{:S(2)}) %copy-start.4) | copy-done | bytes 131096
  9.3 0.0 copy-start.5
  9.3 0.9 %copy-done.5 = bf16[256,256]{1,0:T(8,128)(2,1)S(1)} copy-done((bf16[256,256]{1,0:T(8,128)(2,1)S(1)}, bf16[256,256]{1,0:T(8,128)(2,1)}, u32[]{:S(2)}) %copy-start.5) | copy-done | bytes 131096
  10.2 0.0 copy-start.6
  10.2 0.7 %copy-done.6 = s32[1,4,128]{2,1,0:T(4,128)S(1)} copy-done((s32[1,4,128]{2,1,0:T(4,128)S(1)}, s32[1,4,128]{2,1,0:T(4,128)}, u32[]{:S(2)}) %copy-start.6) | copy-done | bytes 2072
  10.9 0.0 copy-start.9
  10.9 0.7 %copy-done.9 = s32[1,4]{1,0:T(1,128)S(1)} copy-done((s32[1,4]{1,0:T(1,128)S(1)}, s32[1,4]{1,0:T(1,128)}, u32[]{:S(2)}) %copy-start.9) | copy-done | bytes 40
  11.6 25.1 %layer.1 = (bf16[1024,256]{1,0:T(8,128)(2,1)S(1)}, bf16[1024,256]{1,0:T(8,128)(2,1)S(1)}, bf16[512,256]{1,0:T(8,128)(2,1)S(1)}, f32[64,256]{1,0:T(8,128)S(1)}) custom-call(s32[1,4]{1,0:T(1,128)S(1)} %copy-done.9, s32[1,4,128]{2,1,0:T(4,128)S(1)} %copy-done.6, bf16[1536,512]{1,0:T(8,128)(2,1)S(1)} %get-tuple-element.10.adj_hbm, ...), custom_call_target="tpu_custom_call" | custom-call | tf_op jit(solution)/shard_map/layer/pallas_call | solution.py:362
  36.6 1.3 %results.1 = (bf16[1024,256]{1,0:T(8,128)(2,1)}, bf16[1024,256]{1,0:T(8,128)(2,1)}, bf16[512,256]{1,0:T(8,128)(2,1)}, f32[64,256]{1,0:T(8,128)}) custom-call(bf16[1024,256]{1,0:T(8,128)(2,1)S(1)} %get-tuple-element.12.refs_0_, bf16[1024,256]{1,0:T(8,128)(2,1)S(1)} %get-tuple-element.13.refs_1_, bf16[512,256]{1,0:T(8,128)(2,1)S(1)} %get-tuple-element.14.refs_2_, ...), custom_call_target="tpu_custom_call" | custom-call | tf_op jit(solution)/shard_map/results/pallas_call | solution.py:413
Async XLA Ops:
  1.3 1.0 %copy-start = (bf16[512,256]{1,0:T(8,128)(2,1)S(1)}, bf16[512,256]{1,0:T(8,128)(2,1)}, u32[]{:S(2)}) copy-start(bf16[512,256]{1,0:T(8,128)(2,1)} %x_src_hbm.3) | copy-start | bytes 786436
  2.2 1.1 %copy-start.1 = (bf16[24,128,128]{2,1,0:T(8,128)(2,1)S(1)}, bf16[24,128,128]{2,1,0:T(8,128)(2,1)}, u32[]{:S(2)}) copy-start(bf16[24,128,128]{2,1,0:T(8,128)(2,1)} %tiles_hbm.1) | copy-start | bytes 2359300
  3.4 0.7 %copy-start.7 = (s32[24]{0:T(128)S(1)}, s32[24]{0:T(128)}, u32[]{:S(2)}) copy-start(s32[24]{0:T(128)} %dest_ref.1) | copy-start | bytes 292
  4.0 0.7 %copy-start.8 = (s32[24]{0:T(128)S(1)}, s32[24]{0:T(128)}, u32[]{:S(2)}) copy-start(s32[24]{0:T(128)} %col_ref.1) | copy-start | bytes 292
  6.3 1.0 %copy-start.2 = (bf16[1024,256]{1,0:T(8,128)(2,1)S(1)}, bf16[1024,256]{1,0:T(8,128)(2,1)}, u32[]{:S(2)}) copy-start(bf16[1024,256]{1,0:T(8,128)(2,1)} %x_self_hbm.1) | copy-start | bytes 1572868
  7.4 1.0 %copy-start.3 = (bf16[1024,256]{1,0:T(8,128)(2,1)S(1)}, bf16[1024,256]{1,0:T(8,128)(2,1)}, u32[]{:S(2)}) copy-start(bf16[1024,256]{1,0:T(8,128)(2,1)} %cot_hbm.1) | copy-start | bytes 1572868
  8.4 0.9 %copy-start.4 = (bf16[256,256]{1,0:T(8,128)(2,1)S(1)}, bf16[256,256]{1,0:T(8,128)(2,1)}, u32[]{:S(2)}) copy-start(bf16[256,256]{1,0:T(8,128)(2,1)} %w_self_hbm.1) | copy-start | bytes 393220
  9.3 0.9 %copy-start.5 = (bf16[256,256]{1,0:T(8,128)(2,1)S(1)}, bf16[256,256]{1,0:T(8,128)(2,1)}, u32[]{:S(2)}) copy-start(bf16[256,256]{1,0:T(8,128)(2,1)} %w_neigh_hbm.1) | copy-start | bytes 393220
  10.2 0.7 %copy-start.6 = (s32[1,4,128]{2,1,0:T(4,128)S(1)}, s32[1,4,128]{2,1,0:T(4,128)}, u32[]{:S(2)}) copy-start(s32[1,4,128]{2,1,0:T(4,128)} %index_hbm.1) | copy-start | bytes 6148
  10.9 0.7 %copy-start.9 = (s32[1,4]{1,0:T(1,128)S(1)}, s32[1,4]{1,0:T(1,128)}, u32[]{:S(2)}) copy-start(s32[1,4]{1,0:T(1,128)} %live_ref.1) | copy-start | bytes 52

commit v2 on v1

v2 whole, which is shorter than its diff:
```python
import functools

import jax
import jax.numpy as jnp
from jax import lax
from jax.experimental import pallas as pl
from jax.experimental.pallas import tpu as pltpu
from jax.sharding import PartitionSpec as P

TILE_EDGE = 128
VMEM_LIMIT = 48 * 2**20
MESH = pl.DeviceIdType.MESH
F32 = jnp.float32
BF16 = jnp.bfloat16


def dot(a, b):
    return jnp.dot(a, b, preferred_element_type=F32)


def dot_nt(a, b):
    return lax.dot_general(a, b, (((1,), (1,)), ((), ())), preferred_element_type=F32)


def dot_tn(a, b):
    return lax.dot_general(a, b, (((0,), (0,)), ((), ())), preferred_element_type=F32)


def layer_kernel(
    ndom,
    ngroup,
    capacity,
    factor,
    dest_hbm,
    col_hbm,
    count,
    live_hbm,
    index_hbm,
    tiles_hbm,
    x_src_hbm,
    x_self_hbm,
    cot_hbm,
    w_self_hbm,
    w_neigh_hbm,
    out,
    dx_self,
    dx_src,
    grad_ref,
    dest,
    col,
    live,
    index3,
    index,
    tiles,
    x_src,
    x_self,
    cot,
    w_self,
    w_neigh,
    chosen,
    forward,
    backward,
    pick,
    pick_t,
    mirror,
    own,
    pre_self,
    agg,
    gpre,
    g_rows,
    g_dest,
    mirror_grad,
    received,
    back,
    x_self_t,
    term,
    term_in,
    rows_out,
    rows_in,
    load_sem,
    local_sem,
    send_a,
    recv_a,
    send_b,
    recv_b,
    send_g,
    recv_g,
    send_d,
    recv_d,
):
    me_d = lax.axis_index("dom")
    me_g = lax.axis_index("group")
    masters, width = x_self.shape
    slots = index.shape[1]
    nblock = tiles.shape[0]
    nsrc = dx_src.shape[0]
    grad_rows = term.shape[0] // ngroup
    chunk = 256
    edge = TILE_EDGE
    master_tiles = masters // edge

    barrier = pltpu.get_barrier_semaphore()
    for k in range(1, ndom):
        pl.semaphore_signal(
            barrier, inc=1, device_id={"dom": lax.rem(me_d + k, ndom)}, device_id_type=MESH
        )
    for k in range(1, ngroup):
        pl.semaphore_signal(
            barrier, inc=1, device_id={"group": lax.rem(me_g + k, ngroup)}, device_id_type=MESH
        )
    pairs = [
        (dest_hbm, dest),
        (col_hbm, col),
        (x_src_hbm, x_src),
        (tiles_hbm, tiles),
        (live_hbm, live),
        (index_hbm, index3),
        (x_self_hbm, x_self),
        (w_self_hbm, w_self),
        (w_neigh_hbm, w_neigh),
        (cot_hbm, cot),
    ]
    loads = [pltpu.make_async_copy(a, b, load_sem.at[i]) for i, (a, b) in enumerate(pairs)]
    for load in loads:
        load.start()

    def part(ref, i, rows):
        return ref.at[pl.ds(pl.multiple_of(i * rows, 16), rows), :]

    def exchange(src, dst, rows, size, me, axis, send, recv):
        copies = []
        for k in range(1, size):
            to = lax.rem(me + k, size)
            copy = pltpu.make_async_remote_copy(
                src_ref=part(src, to, rows) if src is not rows_out else src,
                dst_ref=part(dst, me, rows),
                send_sem=send.at[k],
                recv_sem=recv.at[k],
                device_id={axis: to},
                device_id_type=MESH,
            )
            copy.start()
            copies.append(copy)
        return copies

    for load in loads[:4]:
        load.wait()
    row_of, col_of = [], []
    for b in range(nblock):
        alive = (b < count[0]).astype(jnp.int32)
        row_of.append(alive * (dest[b] + 1) - 1)
        col_of.append(alive * (col[b] + 1) - 1)
    for b in range(nblock):
        chosen[b * edge : (b + 1) * edge, :] = x_src[col[b]]

    def kept(tile, key, wanted):
        return tile * jnp.broadcast_to((key == wanted).astype(F32), tile.shape).astype(BF16)

    def spread(at, wanted):
        for b in range(nblock):
            forward[at * edge : (at + 1) * edge, b * edge : (b + 1) * edge] = kept(
                tiles[b], row_of[b], wanted
            )

    for m in range(slots // edge):
        spread(m, master_tiles + m)
    mirror[...] = dot(forward[:slots, :], chosen[...]).astype(BF16)

    pl.semaphore_wait(barrier, ndom + ngroup - 2)
    sent_a = exchange(mirror, received, capacity, ndom, me_d, "dom", send_a, recv_a)
    keep_a = pltpu.make_async_copy(
        part(mirror, me_d, capacity), part(received, me_d, capacity), local_sem.at[0]
    )
    keep_a.start()

    for load in loads[4:]:
        load.wait()
    lane = lax.broadcasted_iota(jnp.int32, (1, capacity), 1)
    for p in range(ndom):
        index[:, p * capacity : (p + 1) * capacity] = jnp.where(
            lane < live[0, p], index3[0, p : p + 1, :], -1
        )
    index_row = index[...]

    for m in range(master_tiles):
        spread(m, m)

    @pl.loop(0, masters // chunk)
    def _(i):
        rows = pl.ds(pl.multiple_of(i * chunk, chunk), chunk)
        own[rows, :] = dot(forward[rows, :], chosen[...])
        pre_self[rows, :] = dot(x_self[rows, :], w_self[...])
        ids = lax.broadcasted_iota(jnp.int32, (chunk, slots), 0) + i * chunk
        pick[rows, :] = jnp.where(ids == index_row, 1.0, 0.0).astype(BF16)

    index_col = jnp.broadcast_to(index_row, (edge, slots)).T
    lanes = lax.broadcasted_iota(jnp.int32, (slots, edge), 1)
    for k in range(masters // edge):
        pick_t[:, k * edge : (k + 1) * edge] = jnp.where(
            lanes + k * edge == index_col, 1.0, 0.0
        ).astype(BF16)
    for k in range(masters // chunk):
        x_self_t[:, k * chunk : (k + 1) * chunk] = x_self[k * chunk : (k + 1) * chunk, :].T

    keep_a.wait()
    for copy in sent_a:
        copy.wait()

    for i in range(masters // chunk):
        rows = pl.ds(i * chunk, chunk)
        agg_rows = (own[rows, :] + dot(pick[rows, :], received[...])).astype(BF16)
        agg[rows, :] = agg_rows
        pre = pre_self[rows, :] + dot(agg_rows, w_neigh[...])
        s = 0.5 * jnp.tanh(0.5 * pre) + 0.5
        value = pre * s
        out[rows, :] = value.astype(BF16)
        g = (cot[rows, :].astype(F32) * (s + value * (1.0 - s))).astype(BF16)
        gpre[rows, :] = g
        g_agg = dot_nt(g, w_neigh[...]).astype(BF16)
        g_rows[rows, :] = g_agg
        for k in range(chunk // edge):
            g_dest[i * chunk // edge + k] = g_agg[k * edge : (k + 1) * edge, :]

    term[:width, :] = dot(x_self_t[...], gpre[...]).astype(BF16)
    term[width:, :] = dot_tn(agg[...], gpre[...]).astype(BF16)
    sent_g = exchange(term, term_in, grad_rows, ngroup, me_g, "group", send_g, recv_g)
    keep_g = pltpu.make_async_copy(
        part(term, me_g, grad_rows), part(term_in, me_g, grad_rows), local_sem.at[2]
    )
    keep_g.start()

    back[...] = dot(pick_t[...], g_rows[...]).astype(BF16)
    sent_b = exchange(back, mirror_grad, capacity, ndom, me_d, "dom", send_b, recv_b)
    keep_b = pltpu.make_async_copy(
        part(back, me_d, capacity),
        part(mirror_grad, me_d, capacity),
        local_sem.at[1],
    )
    keep_b.start()

    @pl.loop(0, masters // chunk)
    def _(i):
        rows = pl.ds(pl.multiple_of(i * chunk, chunk), chunk)
        dx_self[rows, :] = dot_nt(gpre[rows, :], w_self[...]).astype(BF16)

    for b in range(nblock):
        turned = tiles[b].T
        for c in range(nsrc // edge):
            backward[c * edge : (c + 1) * edge, b * edge : (b + 1) * edge] = kept(
                turned, col_of[b], c
            )

    keep_g.wait()
    for copy in sent_g:
        copy.wait()
    total = term_in[:grad_rows, :].astype(F32)
    for j in range(1, ngroup):
        total = total + term_in[j * grad_rows : (j + 1) * grad_rows, :].astype(F32)
    rows_out[...] = total.astype(BF16)
    sent_d = exchange(rows_out, rows_in, grad_rows, ndom, me_d, "dom", send_d, recv_d)
    keep_d = pltpu.make_async_copy(rows_out, part(rows_in, me_d, grad_rows), local_sem.at[3])
    keep_d.start()

    keep_b.wait()
    for copy in sent_b:
        copy.wait()
    for k in range(slots // edge):
        g_dest[master_tiles + k] = mirror_grad[k * edge : (k + 1) * edge, :]
    for b in range(nblock):
        chosen[b * edge : (b + 1) * edge, :] = g_dest[dest[b]]
    dx_src[...] = dot(backward[...], chosen[...]).astype(BF16)

    keep_d.wait()
    for copy in sent_d:
        copy.wait()
    total = rows_in[:grad_rows, :].astype(F32)
    for j in range(1, ndom):
        total = total + rows_in[j * grad_rows : (j + 1) * grad_rows, :].astype(F32)
    grad_ref[...] = total * factor


def results_kernel(*refs):
    sources, targets, sem = refs[:4], refs[4:8], refs[8]
    stores = [pltpu.make_async_copy(a, b, sem.at[i]) for i, (a, b) in enumerate(zip(sources, targets))]
    for store in stores:
        store.start()
    for store in stores:
        store.wait()


def on_device(
    x_self,
    x_src,
    tiles,
    slot_dest_row,
    block_col,
    block_count,
    mirror_count,
    mirror_index,
    cotangent,
    w_self,
    w_neigh,
):
    masters, width = x_self.shape
    nsrc = x_src.shape[0]
    nblock = tiles.shape[0]
    ndom = lax.axis_size("dom")
    ngroup = lax.axis_size("group")
    capacity = mirror_index.shape[2]
    slots = ndom * capacity
    dest = masters + slots
    span = nblock * TILE_EDGE
    grad_rows = 2 * width // ngroup
    vmem = pl.BlockSpec(memory_space=pltpu.VMEM)
    anywhere = pl.BlockSpec(memory_space=pl.ANY)
    hbm = pl.BlockSpec(memory_space=pltpu.HBM)
    factor = float((masters * ngroup * ndom) ** -0.5)

    def rows16(n, m=width):
        return pltpu.VMEM((n, m), BF16)

    def rows32(n, m=width):
        return pltpu.VMEM((n, m), F32)

    def dma(n):
        return pltpu.SemaphoreType.DMA((n,))

    arguments = [
        pltpu.with_memory_space_constraint(a, pltpu.HBM)
        for a in (
            slot_dest_row,
            block_col,
            mirror_count,
            mirror_index,
            tiles,
            x_src.reshape(nsrc // TILE_EDGE, TILE_EDGE, width),
            x_self,
            cotangent,
            w_self,
            w_neigh,
        )
    ]
    arguments.insert(2, block_count)
    in_specs = [hbm] * len(arguments)
    in_specs[2] = pl.BlockSpec(memory_space=pltpu.SMEM)
    result_shapes = (
        jax.ShapeDtypeStruct((masters, width), BF16),
        jax.ShapeDtypeStruct((masters, width), BF16),
        jax.ShapeDtypeStruct((nsrc, width), BF16),
        jax.ShapeDtypeStruct((grad_rows, width), F32),
    )
    results = pl.pallas_call(
        functools.partial(layer_kernel, ndom, ngroup, capacity, factor),
        out_shape=result_shapes,
        in_specs=in_specs,
        out_specs=(vmem,) * 4,
        scratch_shapes=[
            pltpu.SMEM((nblock,), jnp.int32),
            pltpu.SMEM((nblock,), jnp.int32),
            pltpu.SMEM((1, ndom), jnp.int32),
            pltpu.VMEM((1, ndom, capacity), jnp.int32),
            pltpu.VMEM((1, slots), jnp.int32),
            pltpu.VMEM(tiles.shape, BF16),
            pltpu.VMEM((nsrc // TILE_EDGE, TILE_EDGE, width), BF16),
            rows16(masters),
            rows16(masters),
            rows16(width),
            rows16(width),
            rows16(span),
            rows16(max(masters, slots), span),
            rows16(nsrc, span),
            rows16(masters, slots),
            rows16(slots, masters),
            rows16(slots),
            rows32(masters),
            rows32(masters),
            rows16(masters),
            rows16(masters),
            rows16(masters),
            pltpu.VMEM((dest // TILE_EDGE, TILE_EDGE, width), BF16),
            rows16(slots),
            rows16(slots),
            rows16(slots),
            rows16(width, masters),
            rows16(2 * width),
            rows16(2 * width),
            rows16(grad_rows),
            rows16(ndom * grad_rows),
            dma(10),
            dma(4),
            dma(ndom),
            dma(ndom),
            dma(ndom),
            dma(ndom),
            dma(ngroup),
            dma(ngroup),
            dma(ndom),
            dma(ndom),
        ],
        compiler_params=pltpu.CompilerParams(
            collective_id=0, has_side_effects=True, vmem_limit_bytes=VMEM_LIMIT
        ),
        name="layer",
    )(*arguments)
    return pl.pallas_call(
        results_kernel,
        out_shape=result_shapes,
        in_specs=[anywhere] * 4,
        out_specs=(hbm,) * 4,
        scratch_shapes=[dma(4)],
        compiler_params=pltpu.CompilerParams(vmem_limit_bytes=VMEM_LIMIT),
        name="results",
    )(*results)


def solution(mesh):
    return jax.shard_map(
        on_device,
        mesh=mesh,
        in_specs=(
            P(("group", "dom"), None),
            P(("group", "dom"), None),
            P(("group", "dom"), None, None),
            P(("group", "dom")),
            P(("group", "dom")),
            P(("group", "dom")),
            P(("group", "dom"), None),
            P(("group", "dom"), None, None),
            P(("group", "dom"), None),
            P(),
            P(),
        ),
        out_specs=(
            P(("group", "dom"), None),
            P(("group", "dom"), None),
            P(("group", "dom"), None),
            P("group", None),
        ),
        check_vma=False,
    )
```

time: 38.4 us -> 27.1 us (0.71)
  local copies, waits for them, and re-layouts: 8.61 us -> 0 us
  Pallas kernels: 28 us -> 25.6 us
    unnamed x20 -> x0, local copies, waits for them, and re-layouts: 8.61 us -> none
    pallas_call x1 -> x0, Pallas kernels: 1.64 us -> none  [on_device(): pl.pallas_call(functools.partial(adjacency_kernel, masters), out_shape=(j...]
    pallas_call x1, Pallas kernels: 25.1 us -> 24.5 us  [on_device(): pl.pallas_call(functools.partial(layer_kernel, ndom, ngroup, capacity, fa...]
where the time goes in v2:
time: 27.1 us; the launch traced here: 26.9 us
  Pallas kernels  25.6 us (94%)
  between operations  1.29 us (5%)
    pallas_call x1, Pallas kernels, on_device(): pl.pallas_call(functools.partial(layer_kernel, ndom, ngroup, capacity, fa...  24.5 us
    pallas_call x1, Pallas kernels, on_device(): pl.pallas_call(results_kernel, out_shape=result_shapes, in_specs=[anywher...  1.1 us

profile of v2, /device:TPU:0, one launch (start us, length us, event | category | flops | bytes accessed | tf_op | source)
XLA Modules:
  0.0 26.9 jit_solution(12284019003589219329)
XLA Ops:
  1.3 24.5 %layer.1 = (bf16[1024,256]{1,0:T(8,128)(2,1)S(1)}, bf16[1024,256]{1,0:T(8,128)(2,1)S(1)}, bf16[512,256]{1,0:T(8,128)(2,1)S(1)}, f32[64,256]{1,0:T(8,128)S(1)}) custom-call(s32[24]{0:T(128)} %dest_hbm.1, s32[24]{0:T(128)} %col_hbm.1, s32[1]{0:T(128)S(6)} %copy.15.count, s32[1,4]{1,0:T(1,128)} %live_hbm.1, s32[1,4,128]{2,1,0:T(4,128)} %index_hbm.1, ...), custom_call_target="tpu_custom_call" | custom-call | tf_op jit(solution)/shard_map/layer/pallas_call | solution.py:352
  25.8 1.1 %results.1 = (bf16[1024,256]{1,0:T(8,128)(2,1)}, bf16[1024,256]{1,0:T(8,128)(2,1)}, bf16[512,256]{1,0:T(8,128)(2,1)}, f32[64,256]{1,0:T(8,128)}) custom-call(bf16[1024,256]{1,0:T(8,128)(2,1)S(1)} %get-tuple-element.8.refs_0_, bf16[1024,256]{1,0:T(8,128)(2,1)S(1)} %get-tuple-element.9.refs_1_, bf16[512,256]{1,0:T(8,128)(2,1)S(1)} %get-tuple-element.10.refs_2_, ...), custom_call_target="tpu_custom_call" | custom-call | tf_op jit(solution)/shard_map/results/pallas_call | solution.py:405

commit v3 on v2

--- a/solution.py
+++ b/solution.py
@@ -9,6 +9,7 @@
 
 TILE_EDGE = 128
 VMEM_LIMIT = 48 * 2**20
+PARTS = 1
 MESH = pl.DeviceIdType.MESH
 F32 = jnp.float32
 BF16 = jnp.bfloat16
@@ -24,6 +25,15 @@
 
 def dot_tn(a, b):
     return lax.dot_general(a, b, (((0,), (0,)), ((), ())), preferred_element_type=F32)
+
+
+def partner(me, k):
+    bit = 1
+    while bit <= k:
+        if k & bit:
+            me = me + bit - 2 * bit * ((me // bit) % 2)
+        bit *= 2
+    return me
 
 
 def layer_kernel(
@@ -94,19 +104,22 @@
     slots = index.shape[1]
     nblock = tiles.shape[0]
     nsrc = dx_src.shape[0]
+    parts = term_in.shape[0]
     grad_rows = term.shape[0] // ngroup
+    piece = grad_rows // parts
+    half = slots // 2
     chunk = 256
     edge = TILE_EDGE
     master_tiles = masters // edge
 
     barrier = pltpu.get_barrier_semaphore()
-    for k in range(1, ndom):
+    for k in range(ndom - 1, 0, -1):
         pl.semaphore_signal(
-            barrier, inc=1, device_id={"dom": lax.rem(me_d + k, ndom)}, device_id_type=MESH
-        )
-    for k in range(1, ngroup):
+            barrier, inc=1, device_id={"dom": partner(me_d, k)}, device_id_type=MESH
+        )
+    for k in range(ngroup - 1, 0, -1):
         pl.semaphore_signal(
-            barrier, inc=1, device_id={"group": lax.rem(me_g + k, ngroup)}, device_id_type=MESH
+            barrier, inc=1, device_id={"group": partner(me_g, k)}, device_id_type=MESH
         )
     pairs = [
         (dest_hbm, dest),
@@ -127,21 +140,17 @@
     def part(ref, i, rows):
         return ref.at[pl.ds(pl.multiple_of(i * rows, 16), rows), :]
 
-    def exchange(src, dst, rows, size, me, axis, send, recv):
-        copies = []
-        for k in range(1, size):
-            to = lax.rem(me + k, size)
-            copy = pltpu.make_async_remote_copy(
-                src_ref=part(src, to, rows) if src is not rows_out else src,
-                dst_ref=part(dst, me, rows),
-                send_sem=send.at[k],
-                recv_sem=recv.at[k],
-                device_id={axis: to},
-                device_id_type=MESH,
-            )
-            copy.start()
-            copies.append(copy)
-        return copies
+    def send(src, dst, axis, me, k, sent, got):
+        copy = pltpu.make_async_remote_copy(
+            src_ref=src,
+            dst_ref=dst,
+            send_sem=sent,
+            recv_sem=got,
+            device_id={axis: partner(me, k)},
+            device_id_type=MESH,
+        )
+        copy.start()
+        return copy
 
     for load in loads[:4]:
         load.wait()
@@ -167,18 +176,29 @@
     mirror[...] = dot(forward[:slots, :], chosen[...]).astype(BF16)
 
     pl.semaphore_wait(barrier, ndom + ngroup - 2)
-    sent_a = exchange(mirror, received, capacity, ndom, me_d, "dom", send_a, recv_a)
+    sent_a = [None] * ndom
+    for k in [*range(1, ndom // 2), *range(ndom - 1, ndom // 2 - 1, -1)]:
+        sent_a[k] = send(
+            part(mirror, partner(me_d, k), capacity),
+            part(received, k, capacity),
+            "dom",
+            me_d,
+            k,
+            send_a.at[k],
+            recv_a.at[k],
+        )
     keep_a = pltpu.make_async_copy(
-        part(mirror, me_d, capacity), part(received, me_d, capacity), local_sem.at[0]
+        part(mirror, me_d, capacity), part(received, 0, capacity), local_sem.at[0]
     )
     keep_a.start()
 
     for load in loads[4:]:
         load.wait()
     lane = lax.broadcasted_iota(jnp.int32, (1, capacity), 1)
-    for p in range(ndom):
-        index[:, p * capacity : (p + 1) * capacity] = jnp.where(
-            lane < live[0, p], index3[0, p : p + 1, :], -1
+    for k in range(ndom):
+        p = partner(me_d, k)
+        index[:, k * capacity : (k + 1) * capacity] = jnp.where(
+            lane < live[0, p], index3[0, pl.ds(p, 1), :], -1
         )
     index_row = index[...]
 
@@ -203,38 +223,71 @@
         x_self_t[:, k * chunk : (k + 1) * chunk] = x_self[k * chunk : (k + 1) * chunk, :].T
 
     keep_a.wait()
-    for copy in sent_a:
-        copy.wait()
+    for k in range(1, ndom // 2):
+        sent_a[k].wait()
+
+    @pl.loop(0, masters // chunk)
+    def _(i):
+        rows = pl.ds(pl.multiple_of(i * chunk, chunk), chunk)
+        own[rows, :] += dot(pick[rows, :half], received[:half, :])
+
+    for k in range(ndom // 2, ndom):
+        sent_a[k].wait()
 
     for i in range(masters // chunk):
         rows = pl.ds(i * chunk, chunk)
-        agg_rows = (own[rows, :] + dot(pick[rows, :], received[...])).astype(BF16)
-        agg[rows, :] = agg_rows
-        pre = pre_self[rows, :] + dot(agg_rows, w_neigh[...])
+        agg[rows, :] = (own[rows, :] + dot(pick[rows, half:], received[half:, :])).astype(BF16)
+    for i in range(masters // chunk):
+        rows = pl.ds(i * chunk, chunk)
+        pre = pre_self[rows, :] + dot(agg[rows, :], w_neigh[...])
         s = 0.5 * jnp.tanh(0.5 * pre) + 0.5
         value = pre * s
         out[rows, :] = value.astype(BF16)
-        g = (cot[rows, :].astype(F32) * (s + value * (1.0 - s))).astype(BF16)
-        gpre[rows, :] = g
-        g_agg = dot_nt(g, w_neigh[...]).astype(BF16)
+        gpre[rows, :] = (cot[rows, :].astype(F32) * (s + value * (1.0 - s))).astype(BF16)
+
+    term[:width, :] = dot(x_self_t[...], gpre[...]).astype(BF16)
+    term[width:, :] = dot_tn(agg[...], gpre[...]).astype(BF16)
+
+    def piece_of(ref, i, j):
+        return ref.at[pl.ds(pl.multiple_of(i * grad_rows + j * piece, 16), piece), :]
+
+    sent_g = [
+        [
+            send(
+                piece_of(term, partner(me_g, k), j),
+                part(term_in.at[j], k, piece),
+                "group",
+                me_g,
+                k,
+                send_g.at[j, k],
+                recv_g.at[j, k],
+            )
+            for k in range(ngroup - 1, 0, -1)
+        ]
+        for j in range(parts)
+    ]
+
+    for i in range(masters // chunk):
+        rows = pl.ds(i * chunk, chunk)
+        g_agg = dot_nt(gpre[rows, :], w_neigh[...]).astype(BF16)
         g_rows[rows, :] = g_agg
         for k in range(chunk // edge):
             g_dest[i * chunk // edge + k] = g_agg[k * edge : (k + 1) * edge, :]
-
-    term[:width, :] = dot(x_self_t[...], gpre[...]).astype(BF16)
-    term[width:, :] = dot_tn(agg[...], gpre[...]).astype(BF16)
-    sent_g = exchange(term, term_in, grad_rows, ngroup, me_g, "group", send_g, recv_g)
-    keep_g = pltpu.make_async_copy(
-        part(term, me_g, grad_rows), part(term_in, me_g, grad_rows), local_sem.at[2]
-    )
-    keep_g.start()
-
     back[...] = dot(pick_t[...], g_rows[...]).astype(BF16)
-    sent_b = exchange(back, mirror_grad, capacity, ndom, me_d, "dom", send_b, recv_b)
+    sent_b = [
+        send(
+            part(back, k, capacity),
+            part(mirror_grad, me_d, capacity),
+            "dom",
+            me_d,
+            k,
+            send_b.at[k],
+            recv_b.at[k],
+        )
+        for k in range(1, ndom)
+    ]
     keep_b = pltpu.make_async_copy(
-        part(back, me_d, capacity),
-        part(mirror_grad, me_d, capacity),
-        local_sem.at[1],
+        part(back, 0, capacity), part(mirror_grad, me_d, capacity), local_sem.at[1]
     )
     keep_b.start()
 
@@ -250,16 +303,30 @@
                 turned, col_of[b], c
             )
 
-    keep_g.wait()
-    for copy in sent_g:
-        copy.wait()
-    total = term_in[:grad_rows, :].astype(F32)
-    for j in range(1, ngroup):
-        total = total + term_in[j * grad_rows : (j + 1) * grad_rows, :].astype(F32)
-    rows_out[...] = total.astype(BF16)
-    sent_d = exchange(rows_out, rows_in, grad_rows, ndom, me_d, "dom", send_d, recv_d)
-    keep_d = pltpu.make_async_copy(rows_out, part(rows_in, me_d, grad_rows), local_sem.at[3])
-    keep_d.start()
+    sent_d = []
+    for j in range(parts):
+        for copy in sent_g[j]:
+            copy.wait_recv()
+        total = piece_of(term, me_g, j)[...].astype(F32)
+        for k in range(1, ngroup):
+            total = total + term_in[j, k * piece : (k + 1) * piece, :].astype(F32)
+        rows_out[j] = total.astype(BF16)
+        part(rows_in.at[j], me_d, piece)[...] = total.astype(BF16)
+        sent_d += [
+            send(
+                rows_out.at[j],
+                part(rows_in.at[j], me_d, piece),
+                "dom",
+                me_d,
+                k,
+                send_d.at[j, k],
+                recv_d.at[j, k],
+            )
+            for k in range(1, ndom)
+        ]
+    for copies in sent_g:
+        for copy in copies:
+            copy.wait_send()
 
     keep_b.wait()
     for copy in sent_b:
@@ -270,13 +337,13 @@
         chosen[b * edge : (b + 1) * edge, :] = g_dest[dest[b]]
     dx_src[...] = dot(backward[...], chosen[...]).astype(BF16)
 
-    keep_d.wait()
     for copy in sent_d:
         copy.wait()
-    total = rows_in[:grad_rows, :].astype(F32)
-    for j in range(1, ndom):
-        total = total + rows_in[j * grad_rows : (j + 1) * grad_rows, :].astype(F32)
-    grad_ref[...] = total * factor
+    for j in range(parts):
+        total = rows_in[j, :piece, :].astype(F32)
+        for k in range(1, ndom):
+            total = total + rows_in[j, k * piece : (k + 1) * piece, :].astype(F32)
+        grad_ref[j * piece : (j + 1) * piece, :] = total * factor
 
 
 def results_kernel(*refs):
@@ -311,6 +378,8 @@
     dest = masters + slots
     span = nblock * TILE_EDGE
     grad_rows = 2 * width // ngroup
+    parts = max(1, min(PARTS, grad_rows // 16))
+    piece = grad_rows // parts
     vmem = pl.BlockSpec(memory_space=pltpu.VMEM)
     anywhere = pl.BlockSpec(memory_space=pl.ANY)
     hbm = pl.BlockSpec(memory_space=pltpu.HBM)
@@ -322,8 +391,8 @@
     def rows32(n, m=width):
         return pltpu.VMEM((n, m), F32)
 
-    def dma(n):
-        return pltpu.SemaphoreType.DMA((n,))
+    def dma(*shape):
+        return pltpu.SemaphoreType.DMA(shape)
 
     arguments = [
         pltpu.with_memory_space_constraint(a, pltpu.HBM)
@@ -383,19 +452,19 @@
             rows16(slots),
             rows16(width, masters),
             rows16(2 * width),
-            rows16(2 * width),
-            rows16(grad_rows),
-            rows16(ndom * grad_rows),
+            pltpu.VMEM((parts, ngroup * piece, width), BF16),
+            pltpu.VMEM((parts, piece, width), BF16),
+            pltpu.VMEM((parts, ndom * piece, width), BF16),
             dma(10),
-            dma(4),
+            dma(2),
             dma(ndom),
             dma(ndom),
             dma(ndom),
             dma(ndom),
-            dma(ngroup),
-            dma(ngroup),
-            dma(ndom),
-            dma(ndom),
+            dma(parts, ngroup),
+            dma(parts, ngroup),
+            dma(parts, ndom),
+            dma(parts, ndom),
         ],
         compiler_params=pltpu.CompilerParams(
             collective_id=0, has_side_effects=True, vmem_limit_bytes=VMEM_LIMIT

time: 27.1 us -> 26.1 us (0.963)
  Pallas kernels: 25.6 us -> 24.6 us
    pallas_call x1, Pallas kernels: 24.5 us -> 23.5 us  [on_device(): pl.pallas_call(functools.partial(layer_kernel, ndom, ngroup, capacity, fa...]
where the time goes in v3:
time: 26.1 us; the launch traced here: 25.9 us
  Pallas kernels  24.6 us (94%)
  between operations  1.29 us (5%)
    pallas_call x1, Pallas kernels, on_device(): pl.pallas_call(functools.partial(layer_kernel, ndom, ngroup, capacity, fa...  23.5 us
    pallas_call x1, Pallas kernels, on_device(): pl.pallas_call(results_kernel, out_shape=result_shapes, in_specs=[anywher...  1.1 us

profile of v3, /device:TPU:0, one launch (start us, length us, event | category | flops | bytes accessed | tf_op | source)
XLA Modules:
  0.0 25.9 jit_solution(5934996936961411961)
XLA Ops:
  1.3 23.5 %layer.1 = (bf16[1024,256]{1,0:T(8,128)(2,1)S(1)}, bf16[1024,256]{1,0:T(8,128)(2,1)S(1)}, bf16[512,256]{1,0:T(8,128)(2,1)S(1)}, f32[64,256]{1,0:T(8,128)S(1)}) custom-call(s32[24]{0:T(128)} %dest_hbm.1, s32[24]{0:T(128)} %col_hbm.1, s32[1]{0:T(128)S(6)} %copy.15.count, s32[1,4]{1,0:T(1,128)} %live_hbm.1, s32[1,4,128]{2,1,0:T(4,128)} %index_hbm.1, ...), custom_call_target="tpu_custom_call" | custom-call | tf_op jit(solution)/shard_map/layer/pallas_call | solution.py:421
  24.8 1.1 %results.1 = (bf16[1024,256]{1,0:T(8,128)(2,1)}, bf16[1024,256]{1,0:T(8,128)(2,1)}, bf16[512,256]{1,0:T(8,128)(2,1)}, f32[64,256]{1,0:T(8,128)}) custom-call(bf16[1024,256]{1,0:T(8,128)(2,1)S(1)} %get-tuple-element.8.refs_0_, bf16[1024,256]{1,0:T(8,128)(2,1)S(1)} %get-tuple-element.9.refs_1_, bf16[512,256]{1,0:T(8,128)(2,1)S(1)} %get-tuple-element.10.refs_2_, ...), custom_call_target="tpu_custom_call" | custom-call | tf_op jit(solution)/shard_map/results/pallas_call | solution.py:474

commit v4 on v3

--- a/solution.py
+++ b/solution.py
@@ -112,15 +112,6 @@
     edge = TILE_EDGE
     master_tiles = masters // edge
 
-    barrier = pltpu.get_barrier_semaphore()
-    for k in range(ndom - 1, 0, -1):
-        pl.semaphore_signal(
-            barrier, inc=1, device_id={"dom": partner(me_d, k)}, device_id_type=MESH
-        )
-    for k in range(ngroup - 1, 0, -1):
-        pl.semaphore_signal(
-            barrier, inc=1, device_id={"group": partner(me_g, k)}, device_id_type=MESH
-        )
     pairs = [
         (dest_hbm, dest),
         (col_hbm, col),
@@ -134,7 +125,19 @@
         (cot_hbm, cot),
     ]
     loads = [pltpu.make_async_copy(a, b, load_sem.at[i]) for i, (a, b) in enumerate(pairs)]
-    for load in loads:
+    for load in loads[:4]:
+        load.start()
+
+    barrier = pltpu.get_barrier_semaphore()
+    for k in range(ndom - 1, 0, -1):
+        pl.semaphore_signal(
+            barrier, inc=1, device_id={"dom": partner(me_d, k)}, device_id_type=MESH
+        )
+    for k in range(ngroup - 1, 0, -1):
+        pl.semaphore_signal(
+            barrier, inc=1, device_id={"group": partner(me_g, k)}, device_id_type=MESH
+        )
+    for load in loads[4:]:
         load.start()
 
     def part(ref, i, rows):
@@ -284,7 +287,7 @@
             send_b.at[k],
             recv_b.at[k],
         )
-        for k in range(1, ndom)
+        for k in [ndom // 2, *[k for i in range(1, ndom // 2) for k in (i, ndom // 2 + i)]]
     ]
     keep_b = pltpu.make_async_copy(
         part(back, 0, capacity), part(mirror_grad, me_d, capacity), local_sem.at[1]

time: 26.1 us -> 26.1 us (level)
  no operation moved by 1% of the time
where the time goes in v4:
time: 26.1 us; the launch traced here: 25.9 us
  Pallas kernels  24.7 us (95%)
  between operations  1.29 us (5%)
    pallas_call x1, Pallas kernels, on_device(): pl.pallas_call(functools.partial(layer_kernel, ndom, ngroup, capacity, fa...  23.6 us
    pallas_call x1, Pallas kernels, on_device(): pl.pallas_call(results_kernel, out_shape=result_shapes, in_specs=[anywher...  1.1 us

profile of v4, /device:TPU:0, one launch (start us, length us, event | category | flops | bytes accessed | tf_op | source)
XLA Modules:
  0.0 25.9 jit_solution(9379367615552654411)
XLA Ops:
  1.3 23.6 %layer.1 = (bf16[1024,256]{1,0:T(8,128)(2,1)S(1)}, bf16[1024,256]{1,0:T(8,128)(2,1)S(1)}, bf16[512,256]{1,0:T(8,128)(2,1)S(1)}, f32[64,256]{1,0:T(8,128)S(1)}) custom-call(s32[24]{0:T(128)} %dest_hbm.1, s32[24]{0:T(128)} %col_hbm.1, s32[1]{0:T(128)S(6)} %copy.15.count, s32[1,4]{1,0:T(1,128)} %live_hbm.1, s32[1,4,128]{2,1,0:T(4,128)} %index_hbm.1, ...), custom_call_target="tpu_custom_call" | custom-call | tf_op jit(solution)/shard_map/layer/pallas_call | solution.py:424
  24.8 1.1 %results.1 = (bf16[1024,256]{1,0:T(8,128)(2,1)}, bf16[1024,256]{1,0:T(8,128)(2,1)}, bf16[512,256]{1,0:T(8,128)(2,1)}, f32[64,256]{1,0:T(8,128)}) custom-call(bf16[1024,256]{1,0:T(8,128)(2,1)S(1)} %get-tuple-element.8.refs_0_, bf16[1024,256]{1,0:T(8,128)(2,1)S(1)} %get-tuple-element.9.refs_1_, bf16[512,256]{1,0:T(8,128)(2,1)S(1)} %get-tuple-element.10.refs_2_, ...), custom_call_target="tpu_custom_call" | custom-call | tf_op jit(solution)/shard_map/results/pallas_call | solution.py:477

commit v5 on v4

--- a/solution.py
+++ b/solution.py
@@ -306,6 +306,16 @@
                 turned, col_of[b], c
             )
 
+    def row_copy(j, i, to, owner):
+        return pltpu.make_async_remote_copy(
+            src_ref=rows_out.at[j],
+            dst_ref=part(rows_in.at[j], owner, piece),
+            send_sem=send_d.at[j, i],
+            recv_sem=recv_d.at[j, owner],
+            device_id={"dom": to},
+            device_id_type=MESH,
+        )
+
     sent_d = []
     for j in range(parts):
         for copy in sent_g[j]:
@@ -315,18 +325,10 @@
             total = total + term_in[j, k * piece : (k + 1) * piece, :].astype(F32)
         rows_out[j] = total.astype(BF16)
         part(rows_in.at[j], me_d, piece)[...] = total.astype(BF16)
-        sent_d += [
-            send(
-                rows_out.at[j],
-                part(rows_in.at[j], me_d, piece),
-                "dom",
-                me_d,
-                k,
-                send_d.at[j, k],
-                recv_d.at[j, k],
-            )
-            for k in range(1, ndom)
-        ]
+        for i in range(ndom - 1):
+            to = i + (i >= me_d).astype(jnp.int32)
+            row_copy(j, i, to, me_d).start()
+            sent_d.append(row_copy(j, i, to, to))
     for copies in sent_g:
         for copy in copies:
             copy.wait_send()

time: 26.1 us -> 25.8 us (0.989)
  Pallas kernels: 24.7 us -> 24.4 us
    pallas_call x1, Pallas kernels: 23.6 us -> 23.3 us  [on_device(): pl.pallas_call(functools.partial(layer_kernel, ndom, ngroup, capacity, fa...]
where the time goes in v5:
time: 25.8 us; the launch traced here: 25.7 us
  Pallas kernels  24.4 us (95%)
  between operations  1.29 us (5%)
    pallas_call x1, Pallas kernels, on_device(): pl.pallas_call(functools.partial(layer_kernel, ndom, ngroup, capacity, fa...  23.3 us
    pallas_call x1, Pallas kernels, on_device(): pl.pallas_call(results_kernel, out_shape=result_shapes, in_specs=[anywher...  1.1 us

profile of v5, /device:TPU:0, one launch (start us, length us, event | category | flops | bytes accessed | tf_op | source)
XLA Modules:
  0.0 25.7 jit_solution(3355520646040889220)
XLA Ops:
  1.3 23.3 %layer.1 = (bf16[1024,256]{1,0:T(8,128)(2,1)S(1)}, bf16[1024,256]{1,0:T(8,128)(2,1)S(1)}, bf16[512,256]{1,0:T(8,128)(2,1)S(1)}, f32[64,256]{1,0:T(8,128)S(1)}) custom-call(s32[24]{0:T(128)} %dest_hbm.1, s32[24]{0:T(128)} %col_hbm.1, s32[1]{0:T(128)S(6)} %copy.15.count, s32[1,4]{1,0:T(1,128)} %live_hbm.1, s32[1,4,128]{2,1,0:T(4,128)} %index_hbm.1, ...), custom_call_target="tpu_custom_call" | custom-call | tf_op jit(solution)/shard_map/layer/pallas_call | solution.py:426
  24.6 1.1 %results.1 = (bf16[1024,256]{1,0:T(8,128)(2,1)}, bf16[1024,256]{1,0:T(8,128)(2,1)}, bf16[512,256]{1,0:T(8,128)(2,1)}, f32[64,256]{1,0:T(8,128)}) custom-call(bf16[1024,256]{1,0:T(8,128)(2,1)S(1)} %get-tuple-element.8.refs_0_, bf16[1024,256]{1,0:T(8,128)(2,1)S(1)} %get-tuple-element.9.refs_1_, bf16[512,256]{1,0:T(8,128)(2,1)S(1)} %get-tuple-element.10.refs_2_, ...), custom_call_target="tpu_custom_call" | custom-call | tf_op jit(solution)/shard_map/results/pallas_call | solution.py:479

commit v6 on v5

--- a/solution.py
+++ b/solution.py
@@ -179,17 +179,30 @@
     mirror[...] = dot(forward[:slots, :], chosen[...]).astype(BF16)
 
     pl.semaphore_wait(barrier, ndom + ngroup - 2)
-    sent_a = [None] * ndom
-    for k in [*range(1, ndom // 2), *range(ndom - 1, ndom // 2 - 1, -1)]:
-        sent_a[k] = send(
-            part(mirror, partner(me_d, k), capacity),
-            part(received, k, capacity),
-            "dom",
-            me_d,
-            k,
-            send_a.at[k],
-            recv_a.at[k],
-        )
+    def mirror_copy(k, to):
+        return pltpu.make_async_remote_copy(
+            src_ref=part(mirror, to, capacity),
+            dst_ref=part(received, k, capacity),
+            send_sem=send_a.at[k],
+            recv_sem=recv_a.at[k],
+            device_id={"dom": to},
+            device_id_type=MESH,
+        )
+
+    low = (me_d < ndom // 2).astype(jnp.int32)
+    near = low * me_d + (1 - low) * (ndom - 1 - me_d)
+    side = 1 - 2 * low
+    for i in range(ndom - 1):
+        both = (i < 2 * near).astype(jnp.int32)
+        away = both * (i // 2 + 1) + (1 - both) * (i - near + 1)
+        turn = both * (1 - 2 * (i % 2)) - (1 - both)
+        to = me_d + turn * side * away
+        k, bit = 0, 1
+        while bit < ndom:
+            k = k + bit * lax.rem(me_d // bit + to // bit, 2)
+            bit *= 2
+        mirror_copy(k, to).start()
+    sent_a = [None] + [mirror_copy(k, partner(me_d, k)) for k in range(1, ndom)]
     keep_a = pltpu.make_async_copy(
         part(mirror, me_d, capacity), part(received, 0, capacity), local_sem.at[0]
     )

time: 25.8 us -> 25.7 us (level)
  no operation moved by 1% of the time
where the time goes in v6:
time: 25.7 us; the launch traced here: 25.5 us
  Pallas kernels  24.2 us (94%)
  between operations  1.29 us (5%)
    pallas_call x1, Pallas kernels, on_device(): pl.pallas_call(functools.partial(layer_kernel, ndom, ngroup, capacity, fa...  23.1 us
    pallas_call x1, Pallas kernels, on_device(): pl.pallas_call(results_kernel, out_shape=result_shapes, in_specs=[anywher...  1.1 us

profile of v6, /device:TPU:0, one launch (start us, length us, event | category | flops | bytes accessed | tf_op | source)
XLA Modules:
  0.0 25.5 jit_solution(2782226169529898026)
XLA Ops:
  1.3 23.1 %layer.1 = (bf16[1024,256]{1,0:T(8,128)(2,1)S(1)}, bf16[1024,256]{1,0:T(8,128)(2,1)S(1)}, bf16[512,256]{1,0:T(8,128)(2,1)S(1)}, f32[64,256]{1,0:T(8,128)S(1)}) custom-call(s32[24]{0:T(128)} %dest_hbm.1, s32[24]{0:T(128)} %col_hbm.1, s32[1]{0:T(128)S(6)} %copy.15.count, s32[1,4]{1,0:T(1,128)} %live_hbm.1, s32[1,4,128]{2,1,0:T(4,128)} %index_hbm.1, ...), custom_call_target="tpu_custom_call" | custom-call | tf_op jit(solution)/shard_map/layer/pallas_call | solution.py:439
  24.4 1.1 %results.1 = (bf16[1024,256]{1,0:T(8,128)(2,1)}, bf16[1024,256]{1,0:T(8,128)(2,1)}, bf16[512,256]{1,0:T(8,128)(2,1)}, f32[64,256]{1,0:T(8,128)}) custom-call(bf16[1024,256]{1,0:T(8,128)(2,1)S(1)} %get-tuple-element.8.refs_0_, bf16[1024,256]{1,0:T(8,128)(2,1)S(1)} %get-tuple-element.9.refs_1_, bf16[512,256]{1,0:T(8,128)(2,1)S(1)} %get-tuple-element.10.refs_2_, ...), custom_call_target="tpu_custom_call" | custom-call | tf_op jit(solution)/shard_map/results/pallas_call | solution.py:492
